TPU v7x, 32 devices: a whole 2x2x4 slice. The times are simulated.
32 devices in a mesh: energy: 4 (over y, core), slab: 8 (over z, x).
Axes of the slice: x: 2, y: 2, z: 4, core: 2. Of those that a mesh axis runs over, the one named last changes fastest.
Arguments:
- energies: float32 [8], P('energy'), may hold values from 2 to 3
- hamiltonian: bfloat16 [8, 512, 512], P('slab'), may hold values from -0.125 to 0.125
- coupling: bfloat16 [8, 512, 512], P('slab'), may hold values from -0.09375 to 0.09375
- coulomb: bfloat16 [8, 512, 512], P('slab', 'energy'), may hold values from 0.19921875 to 1
- offsets: int32 [8], replicated, may hold values from -4 to 4
Outputs:
- green: float32 [8, 8, 512, 512], P('energy', 'slab')
- self_part: bfloat16 [8, 8, 512, 512], P('energy', 'slab')
All inputs are finite; a program needn't handle non-finite values.
Results may differ from a plain program's by a relative error of at most 0.0058.
Values may be sent and summed in bfloat16 or wider, within the bound.
A program may use at most 64 MiB of HBM per device.

v0:
```python
import functools

import jax
import jax.numpy as jnp
from jax import lax
from jax.experimental import pallas as pl
from jax.experimental.pallas import tpu as pltpu
from jax.sharding import PartitionSpec as P

ROUNDS = 2
PASSES = 2
BROAD = 0.3
BF = jnp.bfloat16
F32 = jnp.float32
MESH = pl.DeviceIdType.MESH


def dot_nn(a, b):
    return lax.dot_general(a, b, (((1,), (0,)), ((), ())), preferred_element_type=F32)


def dot_nt(a, b):
    return lax.dot_general(a, b, (((1,), (1,)), ((), ())), preferred_element_type=F32)


def kernel(
    en, inv, off, h_ref, c_ref, v_ref, go, so,
    cb, hb, cbel, ctp, ctbel, gb, gab, gbe, selfp, el, sf, gx, ret, mat, right, inner, res,
    ini_s, ini_r, hal_s, hal_r, a2a_s, a2a_r, bk_s, bk_r, gx_s, gx_r,
):
    ea, sa = lax.axis_size("energy"), lax.axis_size("slab")
    k = c_ref.shape[1]
    ne = el.shape[1]
    nw = off.shape[0]
    rc = v_ref.shape[1]
    half = k // 2
    rb = half
    me_e, me_s = lax.axis_index("energy"), lax.axis_index("slab")
    r = lax.rem(me_s, 2)
    base_s = me_s - r
    partner = base_s + 1 - r
    hh = lax.rem(me_e, 2)
    mate = me_e + 1 - 2 * hh
    flat = me_e * 2 + r
    has_above = base_s + 2 < sa
    has_below = base_s > 0
    energy = en[r]
    ge = inv[r]

    def copy(src, dst, s, q, dev):
        return pltpu.make_async_remote_copy(
            src_ref=src, dst_ref=dst, send_sem=s, recv_sem=q, device_id=dev, device_id_type=MESH
        )

    def peer(delta):
        other = lax.rem(flat + delta, ne)
        return other, other // 2, lax.rem(other, 2)

    up_dev = (me_e, me_s + 2)
    down_dev = (me_e, me_s - 2)
    barrier = pltpu.get_barrier_semaphore()
    for delta in range(1, ne):
        other, oe, orr = peer(delta)
        pl.semaphore_signal(barrier, inc=1, device_id=(oe, base_s + orr), device_id_type=MESH)

    @pl.when(has_above)
    def _():
        pl.semaphore_signal(barrier, inc=1, device_id=up_dev, device_id_type=MESH)

    @pl.when(has_below)
    def _():
        pl.semaphore_signal(barrier, inc=1, device_id=down_dev, device_id_type=MESH)

    cb[r] = c_ref[0]
    hb[r] = h_ref[0]

    @pl.when(jnp.logical_not(has_below))
    def _():
        cbel[...] = jnp.zeros_like(cbel)
        gbe[...] = jnp.zeros_like(gbe)

    @pl.when(jnp.logical_not(has_above))
    def _():
        gab[...] = jnp.zeros_like(gab)

    peers = ne - 1 + has_above.astype(jnp.int32) + has_below.astype(jnp.int32)
    pl.semaphore_wait(barrier, peers)

    mine = pl.ds(pl.multiple_of(hh * half, half), half)
    theirs = pl.ds(pl.multiple_of((1 - hh) * half, half), half)

    def pair_copy(buf, n):
        return copy(buf.at[r, mine], buf.at[r, mine], ini_s.at[n], ini_r.at[n], (me_e, partner))

    def pair_wait(buf, n):
        copy(buf.at[1 - r, mine], buf.at[1 - r, mine], ini_s.at[n], ini_r.at[n], (me_e, partner)).wait_recv()

    def mate_copy(buf, n):
        return copy(buf.at[1 - r, mine], buf.at[1 - r, mine], ini_s.at[n], ini_r.at[n], (mate, me_s))

    def mate_wait(buf, n):
        copy(buf.at[1 - r, theirs], buf.at[1 - r, theirs], ini_s.at[n], ini_r.at[n], (mate, me_s)).wait_recv()

    c1, h1 = pair_copy(cb, 0), pair_copy(hb, 1)
    c1.start()
    pair_wait(cb, 0)
    c2 = mate_copy(cb, 2)
    c2.start()
    h1.start()
    b1 = copy(cb.at[1, mine], cbel.at[mine], ini_s.at[4], ini_r.at[4], up_dev)
    b2 = copy(cbel.at[mine], cbel.at[mine], ini_s.at[5], ini_r.at[5], (mate, me_s))

    @pl.when(has_above)
    def _():
        b1.start()

    mate_wait(cb, 2)

    def rows_loop(body):
        def run(i, carry):
            i0 = pl.multiple_of(i * rb, rb)
            body(pl.ds(i0, rb), i0)
            return carry

        lax.fori_loop(0, k // rb, run, 0)

    def eye(i0):
        row = lax.broadcasted_iota(jnp.int32, (rb, k), 0) + i0
        col = lax.broadcasted_iota(jnp.int32, (rb, k), 1)
        return row, col

    def base(t, rows, i0):
        row, col = eye(i0)
        out = jnp.where(col == row, energy, 0.0)
        out = jnp.where(col == row + half, -BROAD, out)
        out = jnp.where(col == row - half, BROAD, out)
        return out - hb[t, rows].astype(F32)

    def residue(product, i0):
        row, col = eye(i0)
        return (jnp.where(col == row, 2.0, 0.0) - product).astype(BF)

    def transpose(dst, src):
        for j in range(0, k, 128):
            dst[j:j + 128, :] = src[:, j:j + 128].T

    transpose(ctp, cb[0])
    right[...] = (cb[0].astype(F32) * ge).astype(BF)
    inner[...] = (cb[1].astype(F32) * ge).astype(BF)
    keep = jnp.where(has_above, 1.0, 0.0)

    def first_local(rows, i0):
        mat[0, rows] = dot_nt(cb[0, rows], right[...])
        low = dot_nn(ctp[rows], right[...]).astype(BF).astype(F32)
        mat[1, rows] = keep * dot_nt(cb[1, rows], inner[...]) + low

    rows_loop(first_local)
    pair_wait(hb, 1)
    h2 = mate_copy(hb, 3)
    h2.start()

    @pl.when(has_below)
    def _():
        copy(cbel.at[mine], cbel.at[mine], ini_s.at[4], ini_r.at[4], down_dev).wait_recv()
        b2.start()

    mate_wait(hb, 3)

    def first_end(t, total, rows, i0):
        m = (base(t, rows, i0) - total).astype(BF).astype(F32)
        gb[0, t, rows] = (residue(m * ge, i0).astype(F32) * ge).astype(BF)

    def halo(n, slot):
        down = copy(gb.at[slot, 0], gab.at[n], hal_s.at[n, 0], hal_r.at[n, 0], down_dev)
        up = copy(gb.at[slot, 1], gbe.at[n], hal_s.at[n, 1], hal_r.at[n, 1], up_dev)
        return down, up

    def start_up(n, slot):
        @pl.when(has_above)
        def _():
            halo(n, slot)[1].start()

    def start_down(n, slot):
        @pl.when(has_below)
        def _():
            halo(n, slot)[0].start()

    rows_loop(lambda rows, i0: first_end(1, mat[1, rows], rows, i0))
    start_up(0, 0)

    @pl.when(has_below)
    def _():
        copy(cbel.at[theirs], cbel.at[theirs], ini_s.at[5], ini_r.at[5], (mate, me_s)).wait_recv()

    transpose(ctbel, cbel[...])
    right[...] = (cbel[...].astype(F32) * ge).astype(BF)

    def first_below(rows, i0):
        low = dot_nn(ctbel[rows], right[...]).astype(BF).astype(F32)
        first_end(0, mat[0, rows] + low, rows, i0)

    rows_loop(first_below)
    start_down(0, 0)

    def newton(n, use_self, last, send_next):
        def local_a(rows, i0):
            right[rows] = dot_nt(gb[n, 1, rows], cb[0]).astype(BF)
            inner[rows] = dot_nn(gb[n, 0, rows], cb[0]).astype(BF)

        rows_loop(local_a)

        def local_b(rows, i0):
            up = base(0, rows, i0) - dot_nn(cb[0, rows], right[...])
            low = base(1, rows, i0) - dot_nn(ctp[rows], inner[...]).astype(BF).astype(F32)
            if use_self:
                up = up - selfp[0, rows].astype(F32)
                low = low - selfp[1, rows].astype(F32)
            mat[0, rows] = up
            mat[1, rows] = low

        rows_loop(local_b)

        def finish(t, remote):
            def product(rows, i0):
                m = (mat[t, rows] - remote(rows)).astype(BF)
                res[rows] = residue(dot_nn(m, gb[n, t]), i0)

            rows_loop(product)

            def green(rows, i0):
                value = dot_nn(gb[n, t, rows], res[...])
                gb[n + 1, t, rows] = value.astype(BF)
                if last:
                    @pl.when(r == t)
                    def _():
                        go[t, 0, rows] = value

            rows_loop(green)

        @pl.when(has_above)
        def _():
            copy(gab.at[n], gab.at[n], hal_s.at[n, 0], hal_r.at[n, 0], up_dev).wait_recv()

        def remote_a(rows, i0):
            right[rows] = dot_nt(gab[n, rows], cb[1]).astype(BF)

        rows_loop(remote_a)
        finish(1, lambda rows: dot_nn(cb[1, rows], right[...]))
        if send_next:
            start_up(n + 1, n + 1)

        @pl.when(has_below)
        def _():
            copy(gbe.at[n], gbe.at[n], hal_s.at[n, 1], hal_r.at[n, 1], down_dev).wait_recv()

        def remote_b(rows, i0):
            inner[rows] = dot_nn(gbe[n, rows], cbel[...]).astype(BF)

        rows_loop(remote_b)
        finish(0, lambda rows: dot_nn(ctbel[rows], inner[...]).astype(BF).astype(F32))
        if send_next:
            start_down(n + 1, n + 1)

    def count(d):
        total = jnp.float32(0.0)
        for j in range(nw):
            total = total + jnp.where(off[j] == d, 1.0 / nw, 0.0)
        return total

    myrows = pl.ds(pl.multiple_of(me_e * rc, rc), rc)

    def scatter(rd, slot, delta):
        other, oe, orr = peer(delta)
        rows = pl.ds(pl.multiple_of(oe * rc, rc), rc)
        return copy(
            gb.at[slot, orr, rows], el.at[rd, flat], a2a_s.at[rd, other], a2a_r.at[rd, flat],
            (oe, base_s + orr),
        )

    def gather_wait(rd, delta):
        other, oe, orr = peer(delta)
        copy(
            el.at[rd, other], el.at[rd, other], a2a_s.at[rd, other], a2a_r.at[rd, other],
            (oe, base_s + orr),
        ).wait_recv()

    def convolve(rd, slot):
        for delta in range(1, ne):
            scatter(rd, slot, delta).start()
        el[rd, flat] = gb[slot, r, myrows]

        def after():
            for delta in range(1, ne):
                gather_wait(rd, delta)
            top = ne // 2
            ahead = [count(d) for d in range(top + 1)]
            behind = [count(-d) for d in range(top + 1)]
            columns = k // 128

            def tile(i, carry):
                rows = pl.ds(pl.multiple_of((i // columns) * 16, 16), 16)
                cols = pl.ds(pl.multiple_of(lax.rem(i, columns) * 128, 128), 128)
                g = [el[rd, e, rows, cols].astype(F32) for e in range(ne)]
                v = v_ref[0, rows, cols].astype(F32)
                acc = [jnp.zeros((16, 128), F32) for _ in range(ne)]
                for d in range(top + 1):
                    pol = g[0] * g[d]
                    for e in range(1, ne - d):
                        pol = pol + g[e] * g[e + d]
                    scr = v * (1.0 + (4.0 / ne) * pol * v)
                    a = scr * ahead[d]
                    b = scr * behind[d]
                    for e in range(ne):
                        if e - d >= 0:
                            acc[e] = acc[e] + a * g[e - d]
                        if d > 0 and e + d < ne:
                            acc[e] = acc[e] + b * g[e + d]
                for e in range(ne):
                    sf[rd, e, rows, cols] = acc[e].astype(BF)
                return carry

            lax.fori_loop(0, (rc // 16) * columns, tile, 0)

        return after

    newton(0, False, False, False)
    convolve(0, 1)()

    def back(delta):
        other, oe, orr = peer(delta)
        return copy(
            sf.at[0, other], selfp.at[r, myrows], bk_s.at[0, other], bk_r.at[0, flat],
            (oe, base_s + orr),
        )

    start_up(1, 1)
    start_down(1, 1)
    for delta in range(1, ne):
        back(delta).start()
    selfp[r, myrows] = sf[0, flat]
    for delta in range(1, ne):
        other, oe, orr = peer(delta)
        rows = pl.ds(pl.multiple_of(oe * rc, rc), rc)
        copy(
            sf.at[0, other], selfp.at[orr, rows], bk_s.at[0, other], bk_r.at[0, other],
            (oe, base_s + orr),
        ).wait_recv()

    newton(1, True, False, True)
    newton(2, True, True, False)
    finish_last = convolve(1, 3)
    cross = copy(gb.at[3, 1 - r], gx, gx_s, gx_r, (me_e, partner))
    cross.start()
    finish_last()

    def home(delta):
        oe = lax.rem(me_e + delta, ea)
        return copy(
            sf.at[1, pl.ds(oe * 2, 2)], ret.at[:, myrows], bk_s.at[1, oe], bk_r.at[1, me_e],
            (oe, me_s),
        )

    for delta in range(1, ea):
        home(delta).start()
    ret[:, myrows] = sf[1, pl.ds(me_e * 2, 2)]
    cross.wait_recv()

    def widen(rows, i0):
        go[1 - r, 0, rows] = gx[rows].astype(F32)

    rows_loop(widen)
    for delta in range(1, ea):
        oe = lax.rem(me_e + delta, ea)
        rows = pl.ds(pl.multiple_of(oe * rc, rc), rc)
        copy(
            sf.at[1, pl.ds(oe * 2, 2)], ret.at[:, rows], bk_s.at[1, oe], bk_r.at[1, oe], (oe, me_s)
        ).wait_recv()
    so[:, 0] = ret[...]

    for c in (c1, h1, c2, h2, cross):
        c.wait_send()

    @pl.when(has_above)
    def _():
        b1.wait_send()
        for n in range(3):
            halo(n, n)[1].wait_send()

    @pl.when(has_below)
    def _():
        b2.wait_send()
        for n in range(3):
            halo(n, n)[0].wait_send()

    for delta in range(1, ne):
        scatter(0, 1, delta).wait_send()
        scatter(1, 3, delta).wait_send()
        back(delta).wait_send()
    for delta in range(1, ea):
        home(delta).wait_send()


def local(energies, hamiltonian, coupling, coulomb, offsets):
    k = hamiltonian.shape[1]
    rc = coulomb.shape[1]
    ne = energies.shape[0] * lax.axis_size("energy")
    inverse = lax.reduce_precision(1.0 / energies, 8, 7)
    smem = pl.BlockSpec(memory_space=pltpu.SMEM)
    vmem = pl.BlockSpec(memory_space=pltpu.VMEM)
    dma = pltpu.SemaphoreType.DMA

    def buf(*shape, kind=BF):
        return pltpu.VMEM(shape, kind)

    return pl.pallas_call(
        kernel,
        out_shape=(
            jax.ShapeDtypeStruct((2, 1, k, k), F32),
            jax.ShapeDtypeStruct((2, 1, k, k), BF),
        ),
        in_specs=[smem, smem, smem, vmem, vmem, vmem],
        out_specs=(vmem, vmem),
        scratch_shapes=[
            buf(2, k, k), buf(2, k, k), buf(k, k), buf(k, k), buf(k, k),
            buf(4, 2, k, k), buf(3, k, k), buf(3, k, k), buf(2, k, k),
            buf(2, ne, rc, k), buf(2, ne, rc, k), buf(k, k), buf(2, k, k),
            buf(2, k, k, kind=F32), buf(k, k), buf(k, k), buf(k, k),
            dma((6,)), dma((6,)), dma((3, 2)), dma((3, 2)),
            dma((2, ne)), dma((2, ne)), dma((2, ne)), dma((2, ne)), dma, dma,
        ],
        compiler_params=pltpu.CompilerParams(
            collective_id=0, has_side_effects=True, vmem_limit_bytes=48 * 1024 * 1024
        ),
    )(energies, inverse, offsets, hamiltonian, coupling, coulomb)


def solution(mesh):
    placed = (
        P("energy"),
        P("slab", None, None),
        P("slab", None, None),
        P("slab", "energy", None),
        P(),
    )
    return jax.shard_map(
        local,
        mesh=mesh,
        in_specs=placed,
        out_specs=(P("energy", "slab", None, None), P("energy", "slab", None, None)),
        check_vma=False,
    )
```

profile of v0, /device:TPU:3, one launch (start us, length us, event | category | flops | bytes accessed | tf_op | source)
XLA Modules:
  0.0 128.7 jit_solution(15494982977208421374)
XLA Ops:
  0.6 0.7 divide_reduce-precision_fusion.inv
  1.3 0.0 copy-start
  1.3 1.0 copy-done
  2.3 0.0 copy-start.1
  2.3 1.0 copy-done.1
  3.4 0.0 copy-start.2
  3.4 0.9 copy-done.2
  4.3 0.0 copy-start.3
  4.3 0.7 copy-done.3
  4.9 0.0 copy-start.4
  4.9 0.7 copy-done.4
  5.6 120.8 %shard_map.68 = (f32[2,1,512,512]{3,2,1,0:T(8,128)S(1)}, bf16[2,1,512,512]{3,2,1,0:T(8,128)(2,1)S(1)}) custom-call(f32[2]{0:T(128)S(1)} %copy-done.3, f32[2]{0:T(128)S(1)} %divide_reduce-precision_fusion.inv, s32[8]{0:T(128)S(1)} %copy-done.4, bf16[1,512,512]{2,1,0:T(8,128)(2,1)S(1)} %copy-done, bf16[1,512,512]{2,1,0:T(8,128)(2,1)S(1)} %copy-done.1, ...), custom_call_target="tpu_custom_call" | custom-call | tf_op jit(solution)/shard_map/pallas_call | solution.py:415
  126.4 1.3 %copy.9 = f32[2,1,512,512]{3,2,1,0:T(8,128)} copy(f32[2,1,512,512]{3,2,1,0:T(8,128)S(1)} %get-tuple-element.4) | data formatting | bytes 4194304
  127.7 1.0 copy.10
Async XLA Ops:
  1.3 1.0 copy-start
  2.3 1.0 copy-start.1
  3.4 0.9 copy-start.2
  4.3 0.7 copy-start.3
  4.9 0.7 copy-start.4
where the time goes:
time: 130 us; the launch traced here: 129 us
  Pallas kernels  121 us (93%)
  local copies, waits for them, and re-layouts  6.59 us (5%)
    pallas_call x1, Pallas kernels, local(): pl.pallas_call(kernel, out_shape=(jax.ShapeDtypeStruct((2, 1, k, k), F32)...  121 us
    unnamed x12, local copies, waits for them, and re-layouts  6.59 us

commit v1 on v0

--- a/solution.py
+++ b/solution.py
@@ -24,14 +24,13 @@
 
 
 def kernel(
-    en, inv, off, h_ref, c_ref, v_ref, go, so,
+    nw, pack, h_ref, c_ref, v_ref, go, so,
     cb, hb, cbel, ctp, ctbel, gb, gab, gbe, selfp, el, sf, gx, ret, mat, right, inner, res,
-    ini_s, ini_r, hal_s, hal_r, a2a_s, a2a_r, bk_s, bk_r, gx_s, gx_r,
+    vb, loc, ini_s, ini_r, hal_s, hal_r, a2a_s, a2a_r, bk_s, bk_r, gx_s, gx_r,
 ):
     ea, sa = lax.axis_size("energy"), lax.axis_size("slab")
     k = c_ref.shape[1]
     ne = el.shape[1]
-    nw = off.shape[0]
     rc = v_ref.shape[1]
     half = k // 2
     rb = half
@@ -44,8 +43,8 @@
     flat = me_e * 2 + r
     has_above = base_s + 2 < sa
     has_below = base_s > 0
-    energy = en[r]
-    ge = inv[r]
+    energy = pack[r]
+    ge = pack[2 + r]
 
     def copy(src, dst, s, q, dev):
         return pltpu.make_async_remote_copy(
@@ -71,8 +70,12 @@
     def _():
         pl.semaphore_signal(barrier, inc=1, device_id=down_dev, device_id_type=MESH)
 
-    cb[r] = c_ref[0]
-    hb[r] = h_ref[0]
+    own_c = pltpu.make_async_copy(c_ref.at[0], cb.at[r], loc.at[0])
+    own_h = pltpu.make_async_copy(h_ref.at[0], hb.at[r], loc.at[1])
+    own_v = pltpu.make_async_copy(v_ref.at[0], vb, loc.at[2])
+    own_c.start()
+    own_h.start()
+    own_v.start()
 
     @pl.when(jnp.logical_not(has_below))
     def _():
@@ -89,8 +92,8 @@
     mine = pl.ds(pl.multiple_of(hh * half, half), half)
     theirs = pl.ds(pl.multiple_of((1 - hh) * half, half), half)
 
-    def pair_copy(buf, n):
-        return copy(buf.at[r, mine], buf.at[r, mine], ini_s.at[n], ini_r.at[n], (me_e, partner))
+    def pair_copy(src, buf, n):
+        return copy(src.at[0, mine], buf.at[r, mine], ini_s.at[n], ini_r.at[n], (me_e, partner))
 
     def pair_wait(buf, n):
         copy(buf.at[1 - r, mine], buf.at[1 - r, mine], ini_s.at[n], ini_r.at[n], (me_e, partner)).wait_recv()
@@ -101,19 +104,26 @@
     def mate_wait(buf, n):
         copy(buf.at[1 - r, theirs], buf.at[1 - r, theirs], ini_s.at[n], ini_r.at[n], (mate, me_s)).wait_recv()
 
-    c1, h1 = pair_copy(cb, 0), pair_copy(hb, 1)
+    c1, h1 = pair_copy(c_ref, cb, 0), pair_copy(h_ref, hb, 1)
     c1.start()
+    b0 = copy(c_ref.at[0, mine], cbel.at[mine], ini_s.at[4], ini_r.at[4], up_dev)
+    b1 = copy(cb.at[1, mine], cbel.at[mine], ini_s.at[4], ini_r.at[4], up_dev)
+    b2 = copy(cbel.at[mine], cbel.at[mine], ini_s.at[5], ini_r.at[5], (mate, me_s))
+
+    @pl.when(jnp.logical_and(has_above, r == 1))
+    def _():
+        b0.start()
+
     pair_wait(cb, 0)
     c2 = mate_copy(cb, 2)
     c2.start()
     h1.start()
-    b1 = copy(cb.at[1, mine], cbel.at[mine], ini_s.at[4], ini_r.at[4], up_dev)
-    b2 = copy(cbel.at[mine], cbel.at[mine], ini_s.at[5], ini_r.at[5], (mate, me_s))
-
-    @pl.when(has_above)
+
+    @pl.when(jnp.logical_and(has_above, r == 0))
     def _():
         b1.start()
 
+    own_c.wait()
     mate_wait(cb, 2)
 
     def rows_loop(body):
@@ -165,6 +175,7 @@
         b2.start()
 
     mate_wait(hb, 3)
+    own_h.wait()
 
     def first_end(t, total, rows, i0):
         m = (base(t, rows, i0) - total).astype(BF).astype(F32)
@@ -202,7 +213,7 @@
     rows_loop(first_below)
     start_down(0, 0)
 
-    def newton(n, use_self, last, send_next):
+    def local_part(n):
         def local_a(rows, i0):
             right[rows] = dot_nt(gb[n, 1, rows], cb[0]).astype(BF)
             inner[rows] = dot_nn(gb[n, 0, rows], cb[0]).astype(BF)
@@ -210,44 +221,23 @@
         rows_loop(local_a)
 
         def local_b(rows, i0):
-            up = base(0, rows, i0) - dot_nn(cb[0, rows], right[...])
-            low = base(1, rows, i0) - dot_nn(ctp[rows], inner[...]).astype(BF).astype(F32)
-            if use_self:
-                up = up - selfp[0, rows].astype(F32)
-                low = low - selfp[1, rows].astype(F32)
-            mat[0, rows] = up
-            mat[1, rows] = low
+            mat[0, rows] = base(0, rows, i0) - dot_nn(cb[0, rows], right[...])
+            low = dot_nn(ctp[rows], inner[...]).astype(BF).astype(F32)
+            mat[1, rows] = base(1, rows, i0) - low
 
         rows_loop(local_b)
 
-        def finish(t, remote):
-            def product(rows, i0):
-                m = (mat[t, rows] - remote(rows)).astype(BF)
-                res[rows] = residue(dot_nn(m, gb[n, t]), i0)
-
-            rows_loop(product)
-
-            def green(rows, i0):
-                value = dot_nn(gb[n, t, rows], res[...])
-                gb[n + 1, t, rows] = value.astype(BF)
-                if last:
-                    @pl.when(r == t)
-                    def _():
-                        go[t, 0, rows] = value
-
-            rows_loop(green)
-
-        @pl.when(has_above)
-        def _():
-            copy(gab.at[n], gab.at[n], hal_s.at[n, 0], hal_r.at[n, 0], up_dev).wait_recv()
-
-        def remote_a(rows, i0):
-            right[rows] = dot_nt(gab[n, rows], cb[1]).astype(BF)
-
-        rows_loop(remote_a)
-        finish(1, lambda rows: dot_nn(cb[1, rows], right[...]))
-        if send_next:
-            start_up(n + 1, n + 1)
+    def remote_part(n, t):
+        if t == 1:
+            @pl.when(has_above)
+            def _():
+                copy(gab.at[n], gab.at[n], hal_s.at[n, 0], hal_r.at[n, 0], up_dev).wait_recv()
+
+            def remote_a(rows, i0):
+                right[rows] = dot_nt(gab[n, rows], cb[1]).astype(BF)
+
+            rows_loop(remote_a)
+            return lambda rows: dot_nn(cb[1, rows], right[...])
 
         @pl.when(has_below)
         def _():
@@ -257,25 +247,51 @@
             inner[rows] = dot_nn(gbe[n, rows], cbel[...]).astype(BF)
 
         rows_loop(remote_b)
-        finish(0, lambda rows: dot_nn(ctbel[rows], inner[...]).astype(BF).astype(F32))
-        if send_next:
-            start_down(n + 1, n + 1)
+        return lambda rows: dot_nn(ctbel[rows], inner[...]).astype(BF).astype(F32)
+
+    def finish(n, t, term, last):
+        def product(rows, i0):
+            m = (mat[t, rows] - term(rows)).astype(BF)
+            res[rows] = residue(dot_nn(m, gb[n, t]), i0)
+
+        rows_loop(product)
+
+        def green(rows, i0):
+            value = dot_nn(gb[n, t, rows], res[...])
+            gb[n + 1, t, rows] = value.astype(BF)
+            if last:
+                @pl.when(r == t)
+                def _():
+                    go[t, 0, rows] = value
+
+        rows_loop(green)
+
+    def start_halo(n, t):
+        (start_up if t else start_down)(n, n)
+
+    def self_term(t):
+        return lambda rows: selfp[t, rows].astype(F32)
 
     def count(d):
         total = jnp.float32(0.0)
         for j in range(nw):
-            total = total + jnp.where(off[j] == d, 1.0 / nw, 0.0)
+            total = total + jnp.where(pack[4 + j] == d, 1.0 / nw, 0.0)
         return total
 
     myrows = pl.ds(pl.multiple_of(me_e * rc, rc), rc)
 
-    def scatter(rd, slot, delta):
-        other, oe, orr = peer(delta)
-        rows = pl.ds(pl.multiple_of(oe * rc, rc), rc)
-        return copy(
-            gb.at[slot, orr, rows], el.at[rd, flat], a2a_s.at[rd, other], a2a_r.at[rd, flat],
-            (oe, base_s + orr),
-        )
+    def scatter(rd, slot, t, method):
+        for delta in range(ea):
+            oe = lax.rem(me_e + delta, ea)
+            rows = pl.ds(pl.multiple_of(oe * rc, rc), rc)
+            piece = copy(
+                gb.at[slot, t, rows], el.at[rd, flat], a2a_s.at[rd, oe * 2 + t], a2a_r.at[rd, flat],
+                (oe, base_s + t),
+            )
+            if delta == 0:
+                pl.when(r != t)(getattr(piece, method))
+            else:
+                getattr(piece, method)()
 
     def gather_wait(rd, delta):
         other, oe, orr = peer(delta)
@@ -284,47 +300,50 @@
             (oe, base_s + orr),
         ).wait_recv()
 
-    def convolve(rd, slot):
+    def convolve(rd):
+        top = ne // 2
+        ahead = [count(d) for d in range(top + 1)]
+        behind = [count(-d) for d in range(top + 1)]
+        columns = k // 128
+
+        def tile(i, carry):
+            rows = pl.ds(pl.multiple_of((i // columns) * 16, 16), 16)
+            cols = pl.ds(pl.multiple_of(lax.rem(i, columns) * 128, 128), 128)
+            g = [el[rd, e, rows, cols].astype(F32) for e in range(ne)]
+            v = vb[rows, cols].astype(F32)
+            acc = [jnp.zeros((16, 128), F32) for _ in range(ne)]
+            for d in range(top + 1):
+                pol = g[0] * g[d]
+                for e in range(1, ne - d):
+                    pol = pol + g[e] * g[e + d]
+                scr = v * (1.0 + (4.0 / ne) * pol * v)
+                a = scr * ahead[d]
+                b = scr * behind[d]
+                for e in range(ne):
+                    if e - d >= 0:
+                        acc[e] = acc[e] + a * g[e - d]
+                    if d > 0 and e + d < ne:
+                        acc[e] = acc[e] + b * g[e + d]
+            for e in range(ne):
+                sf[rd, e, rows, cols] = acc[e].astype(BF)
+            return carry
+
+        lax.fori_loop(0, (rc // 16) * columns, tile, 0)
+
+    def gather_all(rd):
         for delta in range(1, ne):
-            scatter(rd, slot, delta).start()
-        el[rd, flat] = gb[slot, r, myrows]
-
-        def after():
-            for delta in range(1, ne):
-                gather_wait(rd, delta)
-            top = ne // 2
-            ahead = [count(d) for d in range(top + 1)]
-            behind = [count(-d) for d in range(top + 1)]
-            columns = k // 128
-
-            def tile(i, carry):
-                rows = pl.ds(pl.multiple_of((i // columns) * 16, 16), 16)
-                cols = pl.ds(pl.multiple_of(lax.rem(i, columns) * 128, 128), 128)
-                g = [el[rd, e, rows, cols].astype(F32) for e in range(ne)]
-                v = v_ref[0, rows, cols].astype(F32)
-                acc = [jnp.zeros((16, 128), F32) for _ in range(ne)]
-                for d in range(top + 1):
-                    pol = g[0] * g[d]
-                    for e in range(1, ne - d):
-                        pol = pol + g[e] * g[e + d]
-                    scr = v * (1.0 + (4.0 / ne) * pol * v)
-                    a = scr * ahead[d]
-                    b = scr * behind[d]
-                    for e in range(ne):
-                        if e - d >= 0:
-                            acc[e] = acc[e] + a * g[e - d]
-                        if d > 0 and e + d < ne:
-                            acc[e] = acc[e] + b * g[e + d]
-                for e in range(ne):
-                    sf[rd, e, rows, cols] = acc[e].astype(BF)
-                return carry
-
-            lax.fori_loop(0, (rc // 16) * columns, tile, 0)
-
-        return after
-
-    newton(0, False, False, False)
-    convolve(0, 1)()
+            gather_wait(rd, delta)
+
+    local_part(0)
+    for t in (0, 1):
+        finish(0, t, remote_part(0, t), False)
+        scatter(0, 1, t, "start")
+        start_halo(1, t)
+    el[0, flat] = gb[1, r, myrows]
+    local_part(1)
+    own_v.wait()
+    gather_all(0)
+    convolve(0)
 
     def back(delta):
         other, oe, orr = peer(delta)
@@ -333,11 +352,16 @@
             (oe, base_s + orr),
         )
 
-    start_up(1, 1)
-    start_down(1, 1)
     for delta in range(1, ne):
         back(delta).start()
     selfp[r, myrows] = sf[0, flat]
+    for t in (0, 1):
+        term = remote_part(1, t)
+
+        def add(rows, i0, t=t, term=term):
+            mat[t, rows] = mat[t, rows] - term(rows)
+
+        rows_loop(add)
     for delta in range(1, ne):
         other, oe, orr = peer(delta)
         rows = pl.ds(pl.multiple_of(oe * rc, rc), rc)
@@ -346,12 +370,23 @@
             (oe, base_s + orr),
         ).wait_recv()
 
-    newton(1, True, False, True)
-    newton(2, True, True, False)
-    finish_last = convolve(1, 3)
+    for t in (1, 0):
+        finish(1, t, self_term(t), False)
+        start_halo(2, t)
+    local_part(2)
+    for t in (0, 1):
+        term = remote_part(2, t)
+
+        def whole(rows, t=t, term=term):
+            return selfp[t, rows].astype(F32) + term(rows)
+
+        finish(2, t, whole, True)
+        scatter(1, 3, t, "start")
+    el[1, flat] = gb[3, r, myrows]
     cross = copy(gb.at[3, 1 - r], gx, gx_s, gx_r, (me_e, partner))
+    gather_all(1)
     cross.start()
-    finish_last()
+    convolve(1)
 
     def home(delta):
         oe = lax.rem(me_e + delta, ea)
@@ -393,9 +428,10 @@
             halo(n, n)[0].wait_send()
 
     for delta in range(1, ne):
-        scatter(0, 1, delta).wait_send()
-        scatter(1, 3, delta).wait_send()
         back(delta).wait_send()
+    for t in (0, 1):
+        scatter(0, 1, t, "wait_send")
+        scatter(1, 3, t, "wait_send")
     for delta in range(1, ea):
         home(delta).wait_send()
 
@@ -405,6 +441,8 @@
     rc = coulomb.shape[1]
     ne = energies.shape[0] * lax.axis_size("energy")
     inverse = lax.reduce_precision(1.0 / energies, 8, 7)
+    pack = jnp.concatenate([energies, inverse, offsets.astype(F32)])
+    hbm = pl.BlockSpec(memory_space=pltpu.HBM)
     smem = pl.BlockSpec(memory_space=pltpu.SMEM)
     vmem = pl.BlockSpec(memory_space=pltpu.VMEM)
     dma = pltpu.SemaphoreType.DMA
@@ -413,25 +451,26 @@
         return pltpu.VMEM(shape, kind)
 
     return pl.pallas_call(
-        kernel,
+        functools.partial(kernel, offsets.shape[0]),
         out_shape=(
             jax.ShapeDtypeStruct((2, 1, k, k), F32),
             jax.ShapeDtypeStruct((2, 1, k, k), BF),
         ),
-        in_specs=[smem, smem, smem, vmem, vmem, vmem],
+        in_specs=[smem, hbm, hbm, hbm],
         out_specs=(vmem, vmem),
         scratch_shapes=[
             buf(2, k, k), buf(2, k, k), buf(k, k), buf(k, k), buf(k, k),
             buf(4, 2, k, k), buf(3, k, k), buf(3, k, k), buf(2, k, k),
             buf(2, ne, rc, k), buf(2, ne, rc, k), buf(k, k), buf(2, k, k),
             buf(2, k, k, kind=F32), buf(k, k), buf(k, k), buf(k, k),
+            buf(rc, k), dma((3,)),
             dma((6,)), dma((6,)), dma((3, 2)), dma((3, 2)),
             dma((2, ne)), dma((2, ne)), dma((2, ne)), dma((2, ne)), dma, dma,
         ],
         compiler_params=pltpu.CompilerParams(
             collective_id=0, has_side_effects=True, vmem_limit_bytes=48 * 1024 * 1024
         ),
-    )(energies, inverse, offsets, hamiltonian, coupling, coulomb)
+    )(pack, hamiltonian, coupling, coulomb)
 
 
 def solution(mesh):

time: 130 us -> 119 us (0.915); the launches traced: 129 us -> 119 us
  Pallas kernels: 121 us -> 111 us
  other arithmetic: 0.66 us -> 2.05 us
  local copies, waits for them, and re-layouts: 6.59 us -> 5.28 us
    pallas_call x1, Pallas kernels: 121 us -> 111 us  [local(): pl.pallas_call(functools.partial(kernel, offsets.shape[0]), out_shape=(ja...]
    unnamed x12 -> x8, local copies, waits for them, and re-layouts: 6.59 us -> 5.28 us
where the time goes in v1:
time: 119 us
  Pallas kernels  111 us (93%)
  local copies, waits for them, and re-layouts  5.28 us (4%)
  other arithmetic  2.05 us (2%)
    pallas_call x1, Pallas kernels, local(): pl.pallas_call(functools.partial(kernel, offsets.shape[0]), out_shape=(ja...  111 us
    unnamed x8, local copies, waits for them, and re-layouts  5.28 us

profile of v1, /device:TPU:3, one launch (start us, length us, event | category | flops | bytes accessed | tf_op | source)
XLA Modules:
  0.0 119.1 jit_solution(3433464749344175624)
XLA Ops:
  0.6 0.7 convert_element_type.3
  1.3 0.7 divide_reduce-precision_fusion
  1.9 0.7 pad_maximum_fusion.pack
  2.7 0.0 copy-start
  2.7 1.0 copy-done
  3.7 0.0 copy-start.1
  3.7 1.0 copy-done.1
  4.8 0.0 copy-start.2
  4.8 0.9 copy-done.2
  5.7 111.2 %shard_map.68 = (f32[2,1,512,512]{3,2,1,0:T(8,128)S(1)}, bf16[2,1,512,512]{3,2,1,0:T(8,128)(2,1)S(1)}) custom-call(f32[12]{0:T(128)S(1)} %pad_maximum_fusion.pack, bf16[1,512,512]{2,1,0:T(8,128)(2,1)S(1)} %copy-done, bf16[1,512,512]{2,1,0:T(8,128)(2,1)S(1)} %copy-done.1, bf16[1,128,512]{2,1,0:T(8,128)(2,1)S(1)} %copy-done.2), custom_call_target="tpu_custom_call" | custom-call | tf_op jit(solution)/shard_map/pallas_call | solution.py:453
  116.8 1.3 %copy.9 = f32[2,1,512,512]{3,2,1,0:T(8,128)} copy(f32[2,1,512,512]{3,2,1,0:T(8,128)S(1)} %get-tuple-element.4) | data formatting | bytes 4194304
  118.2 1.0 copy.10
Async XLA Ops:
  2.7 1.0 copy-start
  3.7 1.0 copy-start.1
  4.8 0.9 copy-start.2

commit v2 on v1

--- a/solution.py
+++ b/solution.py
@@ -1,5 +1,3 @@
-import functools
-
 import jax
 import jax.numpy as jnp
 from jax import lax
@@ -24,7 +22,7 @@
 
 
 def kernel(
-    nw, pack, h_ref, c_ref, v_ref, go, so,
+    en, off, h_ref, c_ref, v_ref, go, so,
     cb, hb, cbel, ctp, ctbel, gb, gab, gbe, selfp, el, sf, gx, ret, mat, right, inner, res,
     vb, loc, ini_s, ini_r, hal_s, hal_r, a2a_s, a2a_r, bk_s, bk_r, gx_s, gx_r,
 ):
@@ -33,7 +31,7 @@
     ne = el.shape[1]
     rc = v_ref.shape[1]
     half = k // 2
-    rb = half
+    rb = k
     me_e, me_s = lax.axis_index("energy"), lax.axis_index("slab")
     r = lax.rem(me_s, 2)
     base_s = me_s - r
@@ -43,8 +41,9 @@
     flat = me_e * 2 + r
     has_above = base_s + 2 < sa
     has_below = base_s > 0
-    energy = pack[r]
-    ge = pack[2 + r]
+    nw = off.shape[0]
+    energy = en[r]
+    ge = (1.0 / jnp.full((1, k), energy, F32)).astype(BF).astype(F32)
 
     def copy(src, dst, s, q, dev):
         return pltpu.make_async_remote_copy(
@@ -275,7 +274,7 @@
     def count(d):
         total = jnp.float32(0.0)
         for j in range(nw):
-            total = total + jnp.where(pack[4 + j] == d, 1.0 / nw, 0.0)
+            total = total + jnp.where(off[j] == d, 1.0 / nw, 0.0)
         return total
 
     myrows = pl.ds(pl.multiple_of(me_e * rc, rc), rc)
@@ -440,8 +439,6 @@
     k = hamiltonian.shape[1]
     rc = coulomb.shape[1]
     ne = energies.shape[0] * lax.axis_size("energy")
-    inverse = lax.reduce_precision(1.0 / energies, 8, 7)
-    pack = jnp.concatenate([energies, inverse, offsets.astype(F32)])
     hbm = pl.BlockSpec(memory_space=pltpu.HBM)
     smem = pl.BlockSpec(memory_space=pltpu.SMEM)
     vmem = pl.BlockSpec(memory_space=pltpu.VMEM)
@@ -451,12 +448,12 @@
         return pltpu.VMEM(shape, kind)
 
     return pl.pallas_call(
-        functools.partial(kernel, offsets.shape[0]),
+        kernel,
         out_shape=(
             jax.ShapeDtypeStruct((2, 1, k, k), F32),
             jax.ShapeDtypeStruct((2, 1, k, k), BF),
         ),
-        in_specs=[smem, hbm, hbm, hbm],
+        in_specs=[smem, smem, hbm, hbm, hbm],
         out_specs=(vmem, vmem),
         scratch_shapes=[
             buf(2, k, k), buf(2, k, k), buf(k, k), buf(k, k), buf(k, k),
@@ -468,9 +465,9 @@
             dma((2, ne)), dma((2, ne)), dma((2, ne)), dma((2, ne)), dma, dma,
         ],
         compiler_params=pltpu.CompilerParams(
-            collective_id=0, has_side_effects=True, vmem_limit_bytes=48 * 1024 * 1024
+            collective_id=0, has_side_effects=True, vmem_limit_bytes=60 * 1024 * 1024
         ),
-    )(pack, hamiltonian, coupling, coulomb)
+    )(energies, offsets, hamiltonian, coupling, coulomb)
 
 
 def solution(mesh):

time: 119 us -> 115 us (0.966)
  other arithmetic: 2.05 us -> 0 us
    pallas_call x1, Pallas kernels: 111 us -> 110 us  [local(): pl.pallas_call(kernel, out_shape=(jax.ShapeDtypeStruct((2, 1, k, k), F32)...]
    unnamed x8 -> x4, local copies, waits for them, and re-layouts: 5.28 us -> 4.14 us
where the time goes in v2:
time: 115 us
  Pallas kernels  110 us (96%)
  local copies, waits for them, and re-layouts  4.14 us (4%)
    pallas_call x1, Pallas kernels, local(): pl.pallas_call(kernel, out_shape=(jax.ShapeDtypeStruct((2, 1, k, k), F32)...  110 us
    unnamed x4, local copies, waits for them, and re-layouts  4.14 us

profile of v2, /device:TPU:3, one launch (start us, length us, event | category | flops | bytes accessed | tf_op | source)
XLA Modules:
  0.0 114.6 jit_solution(4845060463654379507)
XLA Ops:
  0.6 109.8 %shard_map.68 = (f32[2,1,512,512]{3,2,1,0:T(8,128)}, bf16[2,1,512,512]{3,2,1,0:T(8,128)(2,1)}) custom-call(f32[2]{0:T(128)} %en.1, s32[8]{0:T(128)} %off.1, bf16[1,512,512]{2,1,0:T(8,128)(2,1)} %h_ref.1, bf16[1,512,512]{2,1,0:T(8,128)(2,1)} %c_ref.1, bf16[1,128,512]{2,1,0:T(8,128)(2,1)} %v_ref.1), custom_call_target="tpu_custom_call" | custom-call | tf_op jit(solution)/shard_map/pallas_call | solution.py:450
  110.5 0.0 copy-start
  110.5 3.2 %copy.9 = f32[2,1,512,512]{3,2,1,0:T(8,128)} copy(f32[2,1,512,512]{3,2,1,0:T(8,128)} %get-tuple-element.4) | data formatting | bytes 4194304
  113.6 0.0 copy-done
  113.6 1.0 copy.10
Async XLA Ops:
  110.5 3.2 %copy-start = (bf16[2,1,512,512]{3,2,1,0:T(8,128)(2,1)S(1)}, bf16[2,1,512,512]{3,2,1,0:T(8,128)(2,1)}, u32[]{:S(2)}) copy-start(bf16[2,1,512,512]{3,2,1,0:T(8,128)(2,1)} %get-tuple-element.5) | copy-start | bytes 3145732
